TPU v7x, 32 devices: a whole 2x2x4 slice. The times are simulated.
32 devices in a mesh: section: 2 (over core), dp: 4 (over y, x), shard: 4 (over z).
Axes of the slice: x: 2, y: 2, z: 4, core: 2. Of those that a mesh axis runs over, the one named last changes fastest.
Arguments:
- boundary: bfloat16 [2, 4, 4, 1024, 1024], P('section', None, 'shard', 'dp'), may hold values from -6 to 6
- first_len: int32 [4, 4], P(None, 'shard'), may hold values from 256 to 1024, as said below
- qkv_weight: bfloat16 [2, 1024, 3072], P('section', 'shard'), may hold values from -0.1875 to 0.1875
- out_weight: bfloat16 [2, 1024, 1024], P('section', 'shard'), may hold values from -0.1875 to 0.1875
- up_weight: bfloat16 [2, 1024, 4096], P('section', 'shard'), may hold values from -0.1875 to 0.1875
- down_weight: bfloat16 [2, 4096, 1024], P('section', 'shard'), may hold values from -0.09375 to 0.09375
- norm_gain: float32 [2, 3, 1024], P('section'), may hold values from 0.5 to 1.5
- norm_shift: float32 [2, 3, 1024], P('section'), may hold values from -1.5 to 1.5
- mid_gain: float32 [2, 4096], P('section'), may hold values from 0.5 to 1.5
- mid_shift: float32 [2, 4096], P('section'), may hold values from -1.5 to 1.5
- head_scale: float32 [2, 16], P('section'), may hold values from 0.25 to 1.75
Outputs:
- ends: bfloat16 [2, 4, 4, 1024, 1024], P('section', None, 'shard', 'dp')
- grad_qkv: float32 [2, 1024, 3072], P('section', 'shard')
- grad_out: float32 [2, 1024, 1024], P('section', 'shard')
- grad_up: float32 [2, 1024, 4096], P('section', 'shard')
- grad_down: float32 [2, 4096, 1024], P('section', 'shard')
- grad_norm_gain: float32 [2, 3, 1024], P('section')
- grad_norm_shift: float32 [2, 3, 1024], P('section')
- grad_mid_gain: float32 [2, 4096], P('section')
- grad_mid_shift: float32 [2, 4096], P('section')
- grad_head_scale: float32 [2, 16], P('section')
Inputs may be any that keep to these rules, and one draw needn't show every extreme that they name: The first document runs from position 0 to first_len - 1 and the second fills the rest of the stream (empty when first_len = 1024). For every stream index g, at least one micro-batch has first_len = 1024.
All inputs are finite; a program needn't handle non-finite values.
Results may differ from a plain program's by a relative error of at most 0.015.
Values may be sent and summed in bfloat16 or wider, within the bound.
A program may use at most 320 MiB of HBM per device.

v0:
```python
import functools
import math
from typing import NamedTuple

import jax
import jax.numpy as jnp
from jax import lax
from jax.experimental import pallas as pl
from jax.experimental.pallas import tpu as pltpu
from jax.sharding import PartitionSpec as P

EPSILON = 1e-05


def shifted(value, axis, steps):
    count = lax.axis_size(axis)
    first, last = (max(0, -steps), min(count, count - steps))
    return lax.ppermute(value, axis, [(source, source + steps) for source in range(first, last)])


def normalize(values_in, gain, shift):
    centre = values_in - jnp.mean(values_in, axis=-1, keepdims=True)
    spread = jnp.mean(centre * centre, axis=-1, keepdims=True)
    return centre * lax.rsqrt(spread + EPSILON) * gain + shift


def middle_norm(hidden, mid_gain, mid_shift):
    return normalize(jax.nn.gelu(hidden, approximate=False), mid_gain, mid_shift)


def contract_rows(left, right):
    return lax.dot_general(
        left, right, (((0,), (0,)), ((), ())), preferred_element_type=jnp.float32
    )


def contract_cols(left, right):
    return lax.dot_general(
        left, right, (((1,), (1,)), ((), ())), preferred_element_type=jnp.float32
    )


def visible(query_place, key_place, split_at):
    same_doc = (query_place[:, None] < split_at) == (key_place[None, :] < split_at)
    return same_doc & (key_place[None, :] <= query_place[:, None])


def forward_parts(stream_in, weights, small, split_at, head_count):
    weight_qkv, weight_out, weight_up, weight_down = weights
    gains, shifts, mid_gain, mid_shift, head_scale = small
    row_count, model_width = stream_in.shape
    head_dim = model_width // head_count
    factor = 1.0 / math.sqrt(head_dim)
    normed = normalize(stream_in, gains[0], shifts[0]).astype(jnp.bfloat16)
    projected = jnp.dot(normed, weight_qkv, preferred_element_type=jnp.float32).astype(jnp.bfloat16)
    queries = projected[:, :model_width].reshape(row_count, head_count, head_dim)
    key_rows = projected[:, model_width : 2 * model_width].reshape(row_count, head_count, head_dim)
    value_rows = projected[:, 2 * model_width :].reshape(row_count, head_count, head_dim)
    keys_all, values_all = (
        lax.all_gather(key_rows, "dp", axis=0, tiled=True),
        lax.all_gather(value_rows, "dp", axis=0, tiled=True),
    )
    seq_len = keys_all.shape[0]
    own_place = lax.axis_index("dp") * row_count + jnp.arange(row_count, dtype=jnp.int32)
    all_place = jnp.arange(seq_len, dtype=jnp.int32)
    allowed = visible(own_place, all_place, split_at)
    scores = (
        jnp.einsum("qhd,khd->hqk", queries, keys_all, preferred_element_type=jnp.float32) * factor
    )
    scores = jnp.where(allowed[None], scores, -1e30)
    row_max = jnp.max(scores, axis=-1, keepdims=True)
    log_total = row_max + jnp.log(jnp.sum(jnp.exp(scores - row_max), axis=-1, keepdims=True))
    attend = jnp.exp(scores - log_total)
    attend_low = attend.astype(jnp.bfloat16)
    head_out = jnp.einsum(
        "hqk,khd->qhd", attend_low, values_all, preferred_element_type=jnp.float32
    )
    scaled = (
        (head_out * head_scale[None, :, None]).astype(jnp.bfloat16).reshape(row_count, model_width)
    )
    branch = jnp.dot(scaled, weight_out, preferred_element_type=jnp.float32)
    residual = stream_in + normalize(branch, gains[1], shifts[1])
    ffn_input = normalize(residual, gains[2], shifts[2]).astype(jnp.bfloat16)
    hidden = jnp.dot(ffn_input, weight_up, preferred_element_type=jnp.float32)
    middle = middle_norm(hidden, mid_gain, mid_shift).astype(jnp.bfloat16)
    return dict(
        normed=normed,
        queries=queries,
        key_rows=key_rows,
        value_rows=value_rows,
        keys_all=keys_all,
        values_all=values_all,
        own_place=own_place,
        all_place=all_place,
        attend=attend,
        attend_low=attend_low,
        log_total=log_total,
        head_out=head_out,
        scaled=scaled,
        branch=branch,
        residual=residual,
        ffn_input=ffn_input,
        hidden=hidden,
        middle=middle,
        factor=factor,
    )


def backward_parts(stream_in, grad_in, weights, small, split_at, head_count):
    weight_qkv, weight_out, weight_up, weight_down = weights
    gains, shifts, mid_gain, mid_shift, head_scale = small
    parts = forward_parts(stream_in, weights, small, split_at, head_count)
    row_count, model_width = stream_in.shape
    head_dim = model_width // head_count
    factor = parts["factor"]
    grad_down = contract_rows(parts["middle"], grad_in)
    d_middle = contract_cols(grad_in, weight_down)
    unused, pull_middle = jax.vjp(middle_norm, parts["hidden"], mid_gain, mid_shift)
    d_hidden, grad_mid_gain, grad_mid_shift = pull_middle(d_middle)
    d_hidden = d_hidden.astype(jnp.bfloat16)
    grad_up = contract_rows(parts["ffn_input"], d_hidden)
    d_ffn_input = contract_cols(d_hidden, weight_up)
    unused, pull_third = jax.vjp(normalize, parts["residual"], gains[2], shifts[2])
    d_residual, gain_third, shift_third = pull_third(d_ffn_input)
    d_residual = d_residual + grad_in.astype(jnp.float32)
    unused, pull_second = jax.vjp(normalize, parts["branch"], gains[1], shifts[1])
    d_branch, gain_second, shift_second = pull_second(d_residual)
    d_branch = d_branch.astype(jnp.bfloat16)
    grad_out = contract_rows(parts["scaled"], d_branch)
    d_scaled = contract_cols(d_branch, weight_out).reshape(row_count, head_count, head_dim)
    grad_head_scale = jnp.sum(d_scaled * parts["head_out"], axis=(0, 2))
    d_heads = (d_scaled * head_scale[None, :, None]).astype(jnp.bfloat16)
    attend = parts["attend"]
    d_attend = jnp.einsum(
        "qhd,khd->hqk", d_heads, parts["values_all"], preferred_element_type=jnp.float32
    )
    row_dot = jnp.sum(attend * d_attend, axis=-1, keepdims=True)
    d_scores = (attend * (d_attend - row_dot)).astype(jnp.bfloat16)
    d_query = (
        jnp.einsum("hqk,khd->qhd", d_scores, parts["keys_all"], preferred_element_type=jnp.float32)
        * factor
    ).astype(jnp.bfloat16)
    full_keys = (
        jnp.einsum("hqk,qhd->khd", d_scores, parts["queries"], preferred_element_type=jnp.float32)
        * factor
    )
    full_values = jnp.einsum(
        "hqk,qhd->khd", parts["attend_low"], d_heads, preferred_element_type=jnp.float32
    )
    d_keys, d_values = (
        lax.psum_scatter(full_keys, "dp", scatter_dimension=0, tiled=True),
        lax.psum_scatter(full_values, "dp", scatter_dimension=0, tiled=True),
    )
    d_projected = jnp.concatenate(
        [
            d_query.reshape(row_count, model_width),
            d_keys.astype(jnp.bfloat16).reshape(row_count, model_width),
            d_values.astype(jnp.bfloat16).reshape(row_count, model_width),
        ],
        axis=1,
    )
    grad_qkv = contract_rows(parts["normed"], d_projected)
    d_normed = contract_cols(d_projected, weight_qkv)
    unused, pull_first = jax.vjp(normalize, stream_in, gains[0], shifts[0])
    d_entry, gain_first, shift_first = pull_first(d_normed)
    d_entry = d_entry + d_residual
    big_grads = (grad_qkv, grad_out, grad_up, grad_down)
    small_grads = (
        jnp.stack([gain_first, gain_second, gain_third]),
        jnp.stack([shift_first, shift_second, shift_third]),
        grad_mid_gain,
        grad_mid_shift,
        grad_head_scale,
    )
    return (d_entry, big_grads, small_grads)


def add_up(first_term, second_term):
    return first_term + second_term


def general(
    boundary,
    first_len,
    qkv_weight,
    out_weight,
    up_weight,
    down_weight,
    norm_gain,
    norm_shift,
    mid_gain,
    mid_shift,
    head_scale,
):
    section_index = lax.axis_index("section")
    gathered = (
        lax.all_gather(qkv_weight, "shard", axis=1, tiled=True),
        lax.all_gather(out_weight, "shard", axis=1, tiled=True),
        lax.all_gather(up_weight, "shard", axis=1, tiled=True),
        lax.all_gather(down_weight, "shard", axis=1, tiled=True),
    )
    weights = tuple((piece[0] for piece in gathered))
    small = (norm_gain[0], norm_shift[0], mid_gain[0], mid_shift[0], head_scale[0])
    head_count = head_scale.shape[1]
    micro = boundary.shape[1]
    row_count = boundary.shape[3]
    model_width = boundary.shape[4]
    local_ends = boundary[0, :, 0]
    splits = first_len[:, 0]

    def forward_tick(step_index, carry):
        incoming, kept, ends = carry
        index = step_index - section_index
        active = (index >= 0) & (index < micro)
        slot = jnp.clip(index, 0, micro - 1)
        entry = jnp.where(section_index == 0, local_ends[slot], incoming)
        parts = forward_parts(entry.astype(jnp.float32), weights, small, splits[slot], head_count)
        result = (
            parts["residual"]
            + jnp.dot(parts["middle"], weights[3], preferred_element_type=jnp.float32)
        ).astype(jnp.bfloat16)
        kept = kept.at[slot].set(jnp.where(active, entry, kept[slot]))
        ends = ends.at[slot].set(jnp.where(active, result, ends[slot]))
        incoming = shifted(result, "section", 1)
        return (incoming, kept, ends)

    blank = jnp.zeros((row_count, model_width), jnp.bfloat16)
    stack_blank = jnp.zeros((micro, row_count, model_width), jnp.bfloat16)
    unused, kept, ends = lax.fori_loop(
        0, micro + 1, forward_tick, (blank, stack_blank, stack_blank)
    )

    def backward_tick(step_index, carry):
        incoming, ends, big_sums, small_sums = carry
        index = micro - step_index - section_index
        active = (index >= 0) & (index < micro)
        slot = jnp.clip(index, 0, micro - 1)
        grad_in = jnp.where(section_index == 1, local_ends[slot], incoming)
        grad_in = jnp.where(active, grad_in, jnp.zeros_like(grad_in))
        d_entry, big_grads, small_grads = backward_parts(
            kept[slot].astype(jnp.float32), grad_in, weights, small, splits[slot], head_count
        )
        d_low = d_entry.astype(jnp.bfloat16)
        ends = ends.at[slot].set(jnp.where(active & (section_index == 0), d_low, ends[slot]))
        big_sums = jax.tree.map(add_up, big_sums, big_grads)
        small_sums = jax.tree.map(add_up, small_sums, small_grads)
        incoming = shifted(d_low, "section", -1)
        return (incoming, ends, big_sums, small_sums)

    big_zero = tuple((jnp.zeros(item.shape, jnp.float32) for item in weights))
    small_zero = tuple((jnp.zeros(item.shape, jnp.float32) for item in small))
    unused, ends, big_sums, small_sums = lax.fori_loop(
        0, micro + 1, backward_tick, (blank, ends, big_zero, small_zero)
    )
    shares = (
        lax.psum_scatter(big_sums[0][None], "shard", scatter_dimension=1, tiled=True),
        lax.psum_scatter(big_sums[1][None], "shard", scatter_dimension=1, tiled=True),
        lax.psum_scatter(big_sums[2][None], "shard", scatter_dimension=1, tiled=True),
        lax.psum_scatter(big_sums[3][None], "shard", scatter_dimension=1, tiled=True),
    )
    shares = lax.psum((shares[0], shares[1], shares[2], shares[3]), "dp")
    totals = lax.psum(
        (small_sums[0], small_sums[1], small_sums[2], small_sums[3], small_sums[4]), ("dp", "shard")
    )
    return (
        ends[None, :, None],
        shares[0],
        shares[1],
        shares[2],
        shares[3],
        totals[0][None],
        totals[1][None],
        totals[2][None],
        totals[3][None],
        totals[4][None],
    )


def pick(value, index):
    return lax.dynamic_index_in_dim(value, index, 0, keepdims=False)


BF16 = jnp.bfloat16
F32 = jnp.float32
TILE = 256
SECTION, DP, SHARD = "section", "dp", "shard"


def rows_spec(columns):
    return pl.BlockSpec((TILE, columns), lambda step: (step, 0))


def group_spec(columns):
    return pl.BlockSpec((4, TILE, columns), lambda step: (0, step, 0))


def array(shape, dtype):
    return jax.ShapeDtypeStruct(shape, dtype)


def dot(left, right):
    return jnp.dot(left, right, preferred_element_type=F32)


def dot_nt(left, right):
    return lax.dot_general(left, right, (((1,), (1,)), ((), ())), preferred_element_type=F32)


def standard(values_in):
    centre = values_in - jnp.mean(values_in, axis=-1, keepdims=True)
    spread_of = jnp.mean(centre * centre, axis=-1, keepdims=True)
    scale = lax.rsqrt(spread_of + EPSILON)
    return centre * scale, scale


def standard_back(unit_values, scale, gain, grad):
    inner = grad * gain
    first = jnp.mean(inner, axis=-1, keepdims=True)
    second = jnp.mean(inner * unit_values, axis=-1, keepdims=True)
    back = scale * (inner - first - unit_values * second)
    return back, jnp.sum(grad * unit_values, axis=0, keepdims=True), jnp.sum(grad, axis=0, keepdims=True)


def lane_masks(rows):
    lanes = lax.broadcasted_iota(jnp.int32, (rows, 128), 1)
    return lanes < 64


def two_columns(first, second):
    return jnp.where(lane_masks(first.shape[0]), first, second)


def mid_stats(own, other):
    mean_own, mean_other = own[:, 0:1], other[:, 0:1]
    gap = mean_own - mean_other
    spread_of = 0.5 * (own[:, 64:65] + other[:, 64:65]) + 0.25 * gap * gap
    return 0.5 * (mean_own + mean_other), lax.rsqrt(spread_of + EPSILON)


def fill_triangle(triangle_ref):
    keys = lax.broadcasted_iota(jnp.int32, (256, 256), 0)
    queries = lax.broadcasted_iota(jnp.int32, (256, 256), 1)
    triangle_ref[...] = jnp.where(keys <= queries, 0.0, -1e30)


def own_lanes(rows, half):
    lane = lax.broadcasted_iota(jnp.int32, (rows, 128), 1)
    return (lane < 64 if half == 0 else lane >= 64), lane == 64 * (1 - half)


def walled_keys(keys, split_at, half):
    mine, spare = own_lanes(1024, half)
    row = lax.broadcasted_iota(jnp.int32, (1024, 128), 0)
    return jnp.where(mine, keys, jnp.where(spare & (row < split_at), -1e30, 0.0).astype(BF16))


def walled_queries(queries, split_at, half, start):
    mine, spare = own_lanes(256, half)
    row = lax.broadcasted_iota(jnp.int32, (256, 128), 0) + start
    return jnp.where(mine, queries, jnp.where(spare & (row >= split_at), 1.0, 0.0).astype(BF16))


def score_parts(keys_ref, queries, block, triangle_ref):
    parts = []
    for part in range(2 * (block + 1)):
        scores = dot_nt(keys_ref[part * 128 : part * 128 + 128, :], queries)
        if part >= 2 * block:
            scores = scores + triangle_ref[(part - 2 * block) * 128 : (part - 2 * block) * 128 + 128, :]
        parts.append(scores)
    return parts


def run_lagged(first, second):
    tasks = [(block, half) for block in (3, 2, 1, 0) for half in (0, 1)]
    before = None
    for task in tasks:
        held = first(*task)
        if before is not None:
            second(*before)
        before = (*task, held)
    second(*before)


def attend(q_ref, k_ref, v_ref, scale_row, out_ref, scaled_ref, log_ref, split_at, triangle_ref, turned_ref, keys_ref):
    turned_ref[...] = v_ref[0].astype(F32).T.astype(BF16)
    for half in range(2):
        keys_ref[half] = walled_keys(k_ref[0], split_at, half)
    found = {}

    def score(block, half):
        queries = (q_ref[0, pl.ds(block * 256, 256), :] * 0.125).astype(BF16)
        parts = score_parts(keys_ref.at[half], walled_queries(queries, split_at, half, block * 256), block, triangle_ref)
        tops = functools.reduce(jnp.maximum, [jnp.max(part.reshape(16, 8, 256), axis=0) for part in parts])
        return parts, jnp.max(tops, axis=0, keepdims=True)

    def mix(block, half, held):
        parts, top = held
        span = pl.ds(block * 256, 256)
        powers = [jnp.exp(part - top) for part in parts]
        total = functools.reduce(jnp.add, [jnp.sum(power.reshape(16, 8, 256), axis=0) for power in powers])
        total = jnp.sum(total, axis=0, keepdims=True)
        low = jnp.concatenate([power.astype(BF16) for power in powers], axis=0)
        mixed = dot(turned_ref[half * 64 : half * 64 + 64, : (block + 1) * 256], low)
        log_ref[0, half : half + 1, span] = top + jnp.log(total)
        found[half] = mixed * (1.0 / total)
        if half == 1:
            head_out = jnp.concatenate([found[0], found[1]], axis=0).T
            out_ref[span, :] = head_out.astype(BF16)
            scaled_ref[span, :] = (head_out * scale_row).astype(BF16)

    run_lagged(score, mix)


def attend_back(
    q_ref, k_ref, v_ref, grad_ref, out_ref, log_ref, back_ref, split_at, triangle_ref, turned_ref, keys_ref, dk_ref, dv_ref
):
    turned_ref[...] = k_ref[0].astype(F32).T.astype(BF16)
    for half in range(2):
        keys_ref[half] = walled_keys(k_ref[0], split_at, half)
    products, found = {}, {}

    def score(block, half):
        span = pl.ds(block * 256, 256)
        mine, unused = own_lanes(256, half)
        queries = (q_ref[0, span, :] * 0.125).astype(BF16)
        grad = grad_ref[span, :]
        own_grad = jnp.where(mine, grad, 0.0).astype(BF16)
        if half == 0:
            products[block] = (grad.astype(F32) * out_ref[span, :].astype(F32)).T
        row_dot = jnp.sum(products[block][half * 64 : half * 64 + 64, :], axis=0, keepdims=True)
        parts = score_parts(keys_ref.at[half], walled_queries(queries, split_at, half, block * 256), block, triangle_ref)
        lows, grads = [], []
        for part, scores in enumerate(parts):
            attend_part = jnp.exp(scores - log_ref[0, half : half + 1, span])
            d_attend = dot_nt(v_ref[0, part * 128 : part * 128 + 128, :], own_grad)
            lows.append(attend_part.astype(BF16))
            grads.append((attend_part * (d_attend - row_dot)).astype(BF16))
        own_queries = jnp.where(mine, queries, 0.0).astype(BF16)
        return jnp.concatenate(lows, axis=0), jnp.concatenate(grads, axis=0), own_queries, own_grad

    def mix(block, half, held):
        low, d_scores, own_queries, own_grad = held
        seen = pl.ds(0, (block + 1) * 256)
        found[half] = dot(turned_ref[half * 64 : half * 64 + 64, : (block + 1) * 256], d_scores)
        if (block, half) == (3, 0):
            dv_ref[...] = dot(low, own_grad)
            dk_ref[...] = dot(d_scores, own_queries)
        else:
            dv_ref[seen, :] += dot(low, own_grad)
            dk_ref[seen, :] += dot(d_scores, own_queries)
        if half == 1:
            d_query = jnp.concatenate([found[0], found[1]], axis=0).T * 0.125
            back_ref[0, pl.ds(block * 256, 256), 0:128] = d_query.astype(BF16)

    run_lagged(score, mix)
    back_ref[0, :, 128:256] = dk_ref[...].astype(BF16)
    back_ref[0, :, 256:384] = dv_ref[...].astype(BF16)


MESH = pl.DeviceIdType.MESH
SIZES = ((256, 384), (128, 256), (256, 512), (512, 256))


def partner(place, step):
    return {0: place, 1: place + 1 - 2 * lax.rem(place, 2), 2: lax.rem(place + 2, 4), 3: 3 - place}[step]


def here():
    return lax.axis_index("section"), lax.axis_index("dp"), lax.axis_index("shard")


def greet(core, place, depth):
    barrier = pltpu.get_barrier_semaphore()
    targets = [{SHARD: lax.rem(depth + step, 4)} for step in (1, 2, 3)]
    targets += [{SECTION: 1 - core, SHARD: lax.rem(depth + step, 4)} for step in range(4)]
    targets += [{DP: partner(place, step)} for step in (1, 2, 3)]
    for target in targets:
        pl.semaphore_signal(barrier, inc=1, device_id=target, device_id_type=MESH)
    pl.semaphore_wait(barrier, len(targets))


def send(source, target, send_sem, recv_sem, device):
    copy = pltpu.make_async_remote_copy(
        src_ref=source, dst_ref=target, send_sem=send_sem, recv_sem=recv_sem,
        device_id=device, device_id_type=MESH,
    )
    copy.start()


def await_bytes(view, sem):
    pltpu.make_async_copy(view, view, sem).wait()


def lanes(start, size):
    return pl.ds(pl.multiple_of(start, 128), size)


def raw_views(raw, matrix, half, quarter):
    if matrix == 0:
        return [raw[0].at[:, lanes(third * 1024 + quarter * 256 + half * 128, 128)] for third in range(3)]
    if matrix == 1:
        return [raw[1].at[pl.ds(half * 128, 128), lanes(quarter * 256, 256)]]
    if matrix == 2:
        return [raw[2].at[:, lanes(quarter * 1024 + half * 512, 512)]]
    return [raw[3].at[pl.ds(half * 512, 512), lanes(quarter * 256, 256)]]


def whole_view(whole, matrix, quarter, shard):
    if matrix in (0, 2):
        return whole[matrix].at[quarter, shard]
    return whole[matrix].at[shard, :, lanes(quarter * 256, 256)]


def whole_views(whole, matrix, quarter, shard):
    if matrix == 0:
        return [whole[0].at[quarter, shard, :, pl.ds(third * 128, 128)] for third in range(3)]
    return [whole_view(whole, matrix, quarter, shard)]


def pieces_view(whole, matrix, first, second):
    if matrix in (0, 2):
        return whole[matrix].at[pl.ds(0, first), pl.ds(0, second)]
    return whole[matrix].at[pl.ds(0, first), :, pl.ds(0, 256 * second)]


class Saved(NamedTuple):
    entry: object
    normed: object
    proj: object
    head_out: object
    scaled: object
    logs: object
    branch: object
    branch_other: object
    residual: object
    ffn_input: object
    gelu: object
    slope: object
    middle: object


def whole_spec(shape):
    return pl.BlockSpec(shape, lambda step: (0,) * len(shape), pipeline_mode=pl.Buffered(1))


def block_spec(rows, columns):
    return pl.BlockSpec((1, rows, columns), lambda step: (step, 0, 0))


def grad_spec(columns):
    return pl.BlockSpec((1, 4, 256, columns), lambda step: (step, 0, 0, 0))


def column_spec(columns):
    return pl.BlockSpec((1024, columns), lambda step: (0, step))


def third_spec(third):
    return pl.BlockSpec((1, 1024, 128), lambda group: (group, 0, third))


def stage(body, ins, outs, hooks=()):
    def hooked(*refs):
        body(*refs)
        for step, action in hooks:
            pl.when(pl.program_id(0) == step)(action)

    pltpu.emit_pipeline(
        hooked, grid=(4,), in_specs=[spec for unused, spec in ins], out_specs=[spec for unused, spec in outs]
    )(*[ref for ref, unused in ins], *[ref for ref, unused in outs])


def after(*actions):
    def run():
        for action, *arguments in actions:
            action(*arguments)

    return run


def block_rows(index):
    return pl.ds(pl.multiple_of(index * 256, 256), 256)


def forward_part(items, raw, small_in, cotangent, wholes, saved, smalls, split_ref, attention_refs, swaps, stats, sems):
    gains, shifts, mid_gain, mid_shift, head_row = smalls
    triangle, turned, walled = attention_refs
    (item_send, item_recv, item_pass, own_send, own_recv, deep_send, deep_recv, hop_send, hop_recv, small_sems,
     swap_send, swap_recv, keep_sem) = sems
    core, place, depth = here()
    arrays = (saved[0].entry, cotangent)
    greet(core, place, depth)

    def items_out(layer):
        @pl.when(core == layer)
        def unused():
            for step in (1, 2, 3):
                send(items.at[partner(place, step)], arrays[layer].at[block_rows(place)], item_send.at[layer, step],
                     item_recv.at[layer, step], {DP: partner(place, step)})
            pltpu.make_async_copy(items.at[place], arrays[layer].at[block_rows(place)], item_send.at[layer, 0]).start()
            send(items.at[place], arrays[layer].at[block_rows(place)], item_pass.at[layer, 0], item_recv.at[layer, 0],
                 {SECTION: 1 - layer})

    def smalls_out():
        for layer in (0, 1):
            @pl.when(core == layer)
            def unused():
                for index, (source, target) in enumerate(zip(small_in, smalls)):
                    pltpu.make_async_copy(source, target.at[layer], small_sems.at[0, index]).start()
                    send(source, target.at[layer], small_sems.at[1, index], small_sems.at[2, index],
                         {SECTION: 1 - layer})

    units = [(layer, matrix) for layer in (0, 1) for matrix in range(4)]

    def deep(unit):
        layer, matrix = units[unit]

        @pl.when(core == layer)
        def unused():
            for step in (1, 2, 3):
                for half in (0, 1):
                    for source, target in zip(
                        raw_views(raw, matrix, half, place), whole_views(wholes[layer], matrix, place, depth)
                    ):
                        send(source, target, deep_send.at[unit], deep_recv.at[unit, step],
                             {SECTION: half, SHARD: lax.rem(depth + 4 - step, 4)})

    def own(unit):
        layer, matrix = units[unit]

        @pl.when(core == layer)
        def unused():
            for quarter in range(4):
                for source, target in zip(
                    raw_views(raw, matrix, layer, quarter), whole_views(wholes[layer], matrix, quarter, depth)
                ):
                    pltpu.make_async_copy(source, target, own_send.at[unit, 0]).start()
                for source, target in zip(
                    raw_views(raw, matrix, 1 - layer, quarter), whole_views(wholes[layer], matrix, quarter, depth)
                ):
                    send(source, target, own_send.at[unit, 1], own_recv.at[unit], {SECTION: 1 - layer})

    def route(unit, step):
        return (1, 2) if (unit + step) % 2 == 0 else (2, 1)

    def piece(unit, offset, step):
        layer, matrix = units[unit]
        return whole_view(wholes[layer], matrix, partner(place, offset), lax.rem(depth + step, 4))

    def first_hop(unit):
        for step in (1, 2, 3):
            first, second = route(unit, step)
            await_bytes(piece(unit, 0, step), deep_recv.at[unit, step])
            for offset in (first, second):
                send(piece(unit, 0, step), piece(unit, 0, step), hop_send.at[unit], hop_recv.at[unit, step - 1, offset - 1],
                     {DP: partner(place, offset)})

    def second_hop(unit):
        for step in (1, 2, 3):
            first, second = route(unit, step)
            await_bytes(piece(unit, first, step), hop_recv.at[unit, step - 1, first - 1])
            send(piece(unit, first, step), piece(unit, first, step), hop_send.at[unit], hop_recv.at[unit, step - 1, 2],
                 {DP: partner(place, second)})

    def ready(unit):
        layer, matrix = units[unit]
        quarters = pieces_view(wholes[layer], matrix, 2, 2)

        @pl.when(core == layer)
        def unused():
            await_bytes(quarters, own_send.at[unit, 0])

        @pl.when(core != layer)
        def unused_too():
            await_bytes(quarters, own_recv.at[unit])

        for step in (1, 2, 3):
            first, second = route(unit, step)
            await_bytes(piece(unit, 0, 0), hop_recv.at[unit, step - 1, second - 1])
            await_bytes(piece(unit, 0, 0), hop_recv.at[unit, step - 1, 2])

    def pass_on(layer):
        @pl.when(core == layer)
        def unused():
            for step in (1, 2, 3):
                block = arrays[layer].at[block_rows(partner(place, step))]
                await_bytes(block, item_recv.at[layer, step])
                send(block, block, item_pass.at[layer, step], item_recv.at[layer, step], {SECTION: 1 - layer})

    def passed(layer):
        @pl.when(core == layer)
        def unused():
            await_bytes(items.at[0], item_send.at[layer, 0])

        @pl.when(core != layer)
        def unused_too():
            for step in range(4):
                await_bytes(items.at[0], item_recv.at[layer, step])

    def take_smalls():
        for index, (source, target) in enumerate(zip(small_in, smalls)):
            for layer in (0, 1):
                @pl.when(core == layer)
                def unused():
                    await_bytes(source, small_sems.at[0, index])

                @pl.when(core != layer)
                def unused_too():
                    await_bytes(source, small_sems.at[2, index])

    def keep(index, source, target):
        pltpu.make_async_copy(source, target, keep_sem.at[index]).start()

    def kept(index, source):
        await_bytes(source, keep_sem.at[index])

    def swap_tile(index, pair, value):
        own_ref, other_ref = pair
        span = block_rows(pl.program_id(0))
        own_ref[span, :] = value
        send(own_ref.at[span], other_ref.at[span], swap_send.at[index], swap_recv.at[index], {SECTION: 1 - core})

    def swapped(index, pair):
        await_bytes(pair[0], swap_send.at[index])
        await_bytes(pair[1], swap_recv.at[index])

    def mid_row(ref, layer, group):
        return ref[layer, :, lanes(group * 1024 + core * 512, 512)]

    def project_rows(layer, x, normed_ref, proj_ref, w_ref):
        unit_x, unused = standard(x)
        normed = (unit_x * gains[layer, 0:1, :] + shifts[layer, 0:1, :]).astype(BF16)
        normed_ref[...] = normed
        for group in range(4):
            proj_ref[group] = dot(normed, w_ref[group].reshape(1024, 384)).astype(BF16)

    def project_stage(layer, hooks):
        own_half = saved[layer]
        weight = (wholes[layer][0], whole_spec((4, 4, 256, 384)))
        made = [(own_half.normed, rows_spec(1024)), (own_half.proj, group_spec(384))]

        def body_first(x_ref, w_ref, normed_ref, proj_ref):
            project_rows(layer, x_ref[...].astype(F32), normed_ref, proj_ref, w_ref)

        def body_next(res_ref, a_ref, b_ref, w_ref, normed_ref, proj_ref, entry_ref):
            entry = (res_ref[...] + (a_ref[...].astype(F32) + b_ref[...].astype(F32))).astype(BF16)
            entry_ref[...] = entry
            project_rows(layer, entry.astype(F32), normed_ref, proj_ref, w_ref)

        if layer == 0:
            stage(body_first, [(own_half.entry, rows_spec(1024)), weight], made, hooks)
        else:
            stage(
                body_next,
                [(saved[0].residual, rows_spec(1024)), (swaps[1][0], rows_spec(1024)), (swaps[1][1], rows_spec(1024)), weight],
                [*made, (own_half.entry, rows_spec(1024))],
                hooks,
            )

    def attention_stage(layer, hooks):
        own_half = saved[layer]

        def body(q_ref, k_ref, v_ref, out_ref, scaled_ref, log_ref):
            scale_row = head_row[layer, :, lanes(pl.program_id(0) * 256 + core * 128, 128)]
            attend(
                q_ref, k_ref, v_ref, scale_row, out_ref, scaled_ref, log_ref, split_ref[0], triangle, turned, walled
            )

        stage(
            body,
            [(own_half.proj, third_spec(0)), (own_half.proj, third_spec(1)), (own_half.proj, third_spec(2))],
            [(own_half.head_out, column_spec(128)), (own_half.scaled, column_spec(128)),
             (own_half.logs, pl.BlockSpec((1, 2, 1024), lambda group: (group, 0, 0)))],
            hooks,
        )

    def out_stage(layer, hooks):
        def body(scaled_ref, w_ref):
            swap_tile(layer * 2, swaps[layer * 2], dot(scaled_ref[...], w_ref[...].reshape(512, 1024)).astype(BF16))

        stage(body, [(saved[layer].scaled, rows_spec(512)), (wholes[layer][1], whole_spec((4, 128, 1024)))], [], hooks)

    def widen_stage(layer, hooks):
        own_half = saved[layer]

        def body(x_ref, a_ref, b_ref, w_ref, res_ref, ffn_ref, gelu_ref, slope_ref):
            branch = a_ref[...].astype(F32) + b_ref[...].astype(F32)
            unit_b, unused = standard(branch)
            residual = x_ref[...].astype(F32) + unit_b * gains[layer, 1:2, :] + shifts[layer, 1:2, :]
            res_ref[...] = residual
            unit_r, unused = standard(residual)
            ffn_input = (unit_r * gains[layer, 2:3, :] + shifts[layer, 2:3, :]).astype(BF16)
            ffn_ref[...] = ffn_input
            first, second = [], []
            for group in range(4):
                hidden = dot(ffn_input, w_ref[group].reshape(1024, 512))
                half = 0.5 + 0.5 * lax.erf(hidden * math.sqrt(0.5))
                gelu = hidden * half
                bell = jnp.exp(-0.5 * hidden * hidden) * (1.0 / math.sqrt(2.0 * math.pi))
                gelu_ref[group] = gelu.astype(BF16)
                slope_ref[group] = (half + hidden * bell).astype(BF16)
                mean = jnp.mean(gelu, axis=-1, keepdims=True)
                centre = gelu - mean
                first.append(mean)
                second.append(jnp.mean(centre * centre, axis=-1, keepdims=True))
            mean = 0.25 * (first[0] + first[1] + first[2] + first[3])
            spread_of = sum(0.25 * (s + (m - mean) * (m - mean)) for m, s in zip(first, second))
            swap_tile(3 + layer, stats[layer], two_columns(mean, spread_of))

        branch_own, branch_other = swaps[layer * 2]
        stage(
            body,
            [(own_half.entry, rows_spec(1024)), (branch_own, rows_spec(1024)), (branch_other, rows_spec(1024)),
             (wholes[layer][2], whole_spec((4, 4, 256, 512)))],
            [(own_half.residual, rows_spec(1024)), (own_half.ffn_input, rows_spec(1024)), (own_half.gelu, group_spec(512)),
             (own_half.slope, group_spec(512))],
            hooks,
        )

    def middle_rows(layer, gelu, mean, scale, group):
        unit_m = (gelu.astype(F32) - mean) * scale
        return (unit_m * mid_row(mid_gain, layer, group) + mid_row(mid_shift, layer, group)).astype(BF16)

    def narrow_stage(layer, hooks):
        own_half = saved[layer]

        def body(g_ref, own_ref, other_ref, w_ref, mid_ref):
            mean, scale = mid_stats(own_ref[...], other_ref[...])
            total = jnp.zeros((TILE, 1024), F32)
            for group in range(4):
                middle = middle_rows(layer, g_ref[group], mean, scale, group)
                mid_ref[group] = middle
                total = total + dot(middle, w_ref[group])
            swap_tile(1, swaps[1], total.astype(BF16))

        stage(
            body,
            [(own_half.gelu, group_spec(512)), (stats[layer][0], rows_spec(128)), (stats[layer][1], rows_spec(128)),
             (wholes[layer][3], whole_spec((4, 512, 1024)))],
            [(own_half.middle, group_spec(512))],
            hooks,
        )

    def middle_stage(layer, hooks):
        own_half = saved[layer]

        def body(g_ref, own_ref, other_ref, mid_ref):
            mean, scale = mid_stats(own_ref[...], other_ref[...])
            for group in range(4):
                mid_ref[group] = middle_rows(layer, g_ref[group], mean, scale, group)

        stage(
            body,
            [(own_half.gelu, group_spec(512)), (stats[layer][0], rows_spec(128)), (stats[layer][1], rows_spec(128))],
            [(own_half.middle, group_spec(512))],
            hooks,
        )

    def layer_forward(layer, hooks, gaps):
        own_half = saved[layer]
        base = layer * 4
        gaps[0]()
        ready(base)
        if layer == 0:
            passed(0)
            take_smalls()
        else:
            swapped(1, swaps[1])
        project_stage(layer, hooks[0])
        attention_stage(layer, hooks[1])
        gaps[1]()
        ready(base + 1)
        out_stage(layer, hooks[2])
        gaps[2]()
        ready(base + 2)
        swapped(layer * 2, swaps[layer * 2])
        for index, (source, target) in enumerate(zip(swaps[layer * 2], (own_half.branch, own_half.branch_other))):
            keep(layer * 2 + index, source, target)
        widen_stage(layer, hooks[3])
        gaps[3]()
        swapped(3 + layer, stats[layer])
        if layer == 0:
            ready(base + 3)
            narrow_stage(layer, hooks[4])
        else:
            middle_stage(layer, hooks[4])

    deep(0)
    items_out(0)
    smalls_out()
    own(0)
    deep(1)
    own(1)
    fill_triangle(triangle)
    first_hop(0)
    deep(2)
    pass_on(0)
    first_hop(1)
    second_hop(0)
    own(2)
    deep(3)
    second_hop(1)
    own(3)
    items_out(1)
    layer_forward(0, ((), ((1, after((first_hop, 2), (deep, 4))),), (), (), ()), (
        after(),
        after((pass_on, 1), (own, 4)),
        after((second_hop, 2), (first_hop, 3), (deep, 5), (own, 5)),
        after((second_hop, 3), (first_hop, 4), (deep, 6), (own, 6)),
    ))
    layer_forward(1, (((1, after((second_hop, 5), (first_hop, 6))),), (), (), (), ()), (
        after((second_hop, 4), (first_hop, 5), (deep, 7), (own, 7)),
        after(),
        after((second_hop, 6), (first_hop, 7)),
        after((second_hop, 7),),
    ))

    for layer in (0, 1):
        for index, source in enumerate(swaps[layer * 2]):
            kept(layer * 2 + index, source)
    passed(1)

    def clean_up():
        for layer in (0, 1):
            @pl.when(core == layer)
            def unused():
                for step in (1, 2, 3):
                    await_bytes(items.at[0], item_send.at[layer, step])
                for step in range(4):
                    await_bytes(items.at[0], item_pass.at[layer, step])
                for index, source in enumerate(small_in):
                    await_bytes(source, small_sems.at[1, index])

        for unit, (layer, matrix) in enumerate(units):
            whole = wholes[layer]

            @pl.when(core == layer)
            def unused_too():
                await_bytes(pieces_view(whole, matrix, 2, 2), own_send.at[unit, 1])
                await_bytes(pieces_view(whole, matrix, 3, 2), deep_send.at[unit])

            await_bytes(pieces_view(whole, matrix, 3, 3), hop_send.at[unit])

    return after((ready, 7)), clean_up


ORDER = tuple((layer, matrix) for layer in (1, 0) for matrix in (3, 2, 1, 0))

class Made(NamedTuple):
    d_middle: object
    d_hidden: object
    d_residual: object
    d_branch: object
    d_heads: object
    d_proj: object
    d_entry: object


def add_up_into(target, *terms):
    rows = target.shape[0]

    def step(index, unused):
        span = pl.ds(pl.multiple_of(index * 32, 32), 32)
        total = target[span, :].astype(F32)
        for term in terms:
            total = total + term[span, :].astype(F32)
        target[span, :] = total.astype(BF16)
        return unused

    lax.fori_loop(0, rows // 32, step, 0)


def whole_kernel(*refs):
    refs = list(refs)

    def take(count):
        found = refs[:count]
        del refs[:count]
        return found

    (split_ref,) = take(1)
    items, *raw = take(5)
    small_in = take(5)
    shares = take(4)
    (ends, small_out) = take(2)
    cotangent, output = take(2)
    weights = (take(4), take(4))
    saved = [Saved(*take(13)) for unused in (0, 1)]
    grads = (take(4), take(4))
    made = [Made(*take(7)) for unused in (0, 1)]
    smalls = take(5)
    attention_refs = take(3)
    swaps = [(*take(2),) for unused in range(3)]
    stats = [(*take(2),) for unused in (0, 1)]
    sums = [(*take(2),) for unused in (0, 1)]
    own, first_in, second_in, deep_in = take(4), take(4), take(4), take(4)
    vec, inbox, acc, dk_acc, dv_acc = take(5)
    forward_sems = take(13)
    (load_sem, first_send, first_recv, second_send, second_recv, deep_send, deep_recv, last_send, last_copy,
     last_recv, ends_send, ends_recv, small_send, small_recv, swap_send, swap_recv, credit) = refs
    gains, unused_shifts, mid_gain, unused_mid_shift, head_row = smalls
    triangle, turned, walled = attention_refs
    core, place, depth = here()
    last_ready, clean_up = forward_part(
        items, raw, small_in, cotangent, weights, saved, smalls, split_ref, attention_refs, swaps, stats, forward_sems
    )

    def send_ends(owner, source):
        @pl.when(core == owner)
        def unused():
            for step in (1, 2, 3):
                send(source.at[block_rows(partner(place, step))], ends.at[place], ends_send.at[step], ends_recv.at[step],
                     {DP: partner(place, step)})
            pltpu.make_async_copy(source.at[block_rows(place)], ends.at[place], ends_send.at[0]).start()

    def route(step):
        return (1, 2) if step < 2 else (2, 1)

    def shard_of(step):
        return lax.rem(depth + step, 4)

    def begin(unit):
        layer, matrix = ORDER[unit]
        if unit >= 4:
            pl.semaphore_wait(credit.at[matrix], 2)
        for step in range(4):
            first, second = route(step)
            for index, offset in enumerate((first, 3)):
                send(whole_view(grads[layer], matrix, partner(place, offset), shard_of(step)),
                     first_in[matrix].at[step, index], first_send.at[unit], first_recv.at[unit],
                     {DP: partner(place, first)})
            for index, offset in enumerate((0, second)):
                pltpu.make_async_copy(
                    whole_view(grads[layer], matrix, partner(place, offset), shard_of(step)),
                    own[matrix].at[step, index], load_sem.at[unit],
                ).start()

    def second_hop(unit):
        layer, matrix = ORDER[unit]
        await_bytes(own[matrix], load_sem.at[unit])
        await_bytes(first_in[matrix], first_recv.at[unit])
        for step in range(4):
            first, second = route(step)
            mine = own[matrix].at[step, 1]
            add_up_into(mine, first_in[matrix].at[step, 1])
            send(mine, second_in[matrix].at[step], second_send.at[unit], second_recv.at[unit],
                 {DP: partner(place, second)})

    def deep_hop(unit):
        layer, matrix = ORDER[unit]
        await_bytes(second_in[matrix], second_recv.at[unit])
        for step in (1, 2, 3, 0):
            mine = own[matrix].at[step, 0]
            add_up_into(mine, first_in[matrix].at[step, 0], second_in[matrix].at[step])
            if step:
                send(mine, deep_in[matrix].at[layer, step - 1], deep_send.at[unit], deep_recv.at[unit],
                     {SHARD: shard_of(step)})
        if unit < 4:
            for step in (1, 2):
                pl.semaphore_signal(
                    credit.at[matrix], inc=1, device_id={DP: partner(place, step)}, device_id_type=MESH
                )

    def finish(unit):
        layer, matrix = ORDER[unit]
        await_bytes(deep_in[matrix].at[layer], deep_recv.at[unit])
        mine = own[matrix].at[0, 0]
        add_up_into(mine, *[deep_in[matrix].at[layer, index] for index in range(3)])
        sources = [mine]
        if matrix == 0:
            sources = [mine.at[:, pl.ds(third * 128, 128)] for third in range(3)]
        for half in (0, 1):
            @pl.when(core == half)
            def unused():
                for source, target in zip(sources, raw_views(shares, matrix, half, place)):
                    if half == layer:
                        pltpu.make_async_copy(source, target, last_copy.at[unit]).start()
                        for offset in (1, 2):
                            send(source, target, last_send.at[unit, 0], last_recv.at[unit, half, offset],
                                 {DP: partner(place, offset)})
                    else:
                        send(source, target, last_send.at[unit, 0], last_recv.at[unit, half, 0], {SECTION: layer})

    def forward(unit):
        layer, matrix = ORDER[unit]
        half = 1 - layer

        @pl.when(core == layer)
        def unused():
            views = raw_views(shares, matrix, half, place)
            await_bytes(own[matrix].at[0, 0], last_recv.at[unit, half, 0])
            for view in views:
                for offset in (1, 2):
                    send(view, view, last_send.at[unit, 1], last_recv.at[unit, half, offset],
                         {DP: partner(place, offset)})

    def corner(unit):
        layer, matrix = ORDER[unit]

        @pl.when(core == layer)
        def unused():
            for half in (layer, 1 - layer):
                first, second = (1, 2) if half == 0 else (2, 1)
                await_bytes(own[matrix].at[0, 0], last_recv.at[unit, half, first])
                for view in raw_views(shares, matrix, half, partner(place, first)):
                    send(view, view, last_send.at[unit, 2], last_recv.at[unit, half, 3], {DP: partner(place, second)})

    def free_own(unit):
        layer, matrix = ORDER[unit]

        @pl.when(core == layer)
        def unused():
            await_bytes(own[matrix].at[0], last_send.at[unit, 0])
            await_bytes(own[matrix].at[0, 0], last_copy.at[unit])

        @pl.when(core != layer)
        def unused_too():
            await_bytes(own[matrix].at[0, 0], last_send.at[unit, 0])

    def free_hops(unit):
        layer, matrix = ORDER[unit]
        await_bytes(second_in[matrix], second_send.at[unit])
        await_bytes(deep_in[matrix].at[layer], deep_send.at[unit])
        free_own(unit)

    def clean(unit):
        layer, matrix = ORDER[unit]
        await_bytes(first_in[matrix], first_send.at[unit])
        if unit >= 4:
            free_hops(unit)

        @pl.when(core == layer)
        def unused():
            for row in (1, 2):
                await_bytes(own[matrix].at[0], last_send.at[unit, row])
            for half in (0, 1):
                first, second = (1, 2) if half == 0 else (2, 1)
                await_bytes(own[matrix].at[0, 0], last_recv.at[unit, half, second])
                await_bytes(own[matrix].at[0, 0], last_recv.at[unit, half, 3])

    column = pl.ds(pl.multiple_of(core * 512, 512), 512)
    exchanges = (
        {SECTION: 1 - core},
        {DP: partner(place, 1)},
        {DP: partner(place, 2)},
        {SHARD: partner(depth, 1)},
        {SHARD: partner(depth, 2)},
    )

    def small_step(index):
        if index:
            send(acc.at[index - 1], inbox.at[index], small_send.at[index], small_recv.at[index], exchanges[index])
        else:
            for layer in (0, 1):
                @pl.when(core != layer)
                def unused():
                    vec[layer, 0:6, :] = jnp.zeros((6, 1024), F32)

            for half in (0, 1):
                @pl.when(core == half)
                def unused_too():
                    send(vec.at[1 - half], inbox.at[0], small_send.at[0], small_recv.at[0], exchanges[0])

    def small_take(index):
        await_bytes(inbox.at[index], small_recv.at[index])
        if index:
            acc[index] = acc[index - 1] + inbox[index]
        else:
            for half in (0, 1):
                @pl.when(core == half)
                def unused():
                    acc[0] = vec[half] + inbox[0]

    def swap_tile(index, pair, value):
        own_ref, other_ref = pair
        span = block_rows(pl.program_id(0))
        own_ref[span, :] = value
        send(own_ref.at[span], other_ref.at[span], swap_send.at[index], swap_recv.at[index], {SECTION: 1 - core})

    def swapped(index, pair):
        await_bytes(pair[0], swap_send.at[index])
        await_bytes(pair[1], swap_recv.at[index])

    def mid_row(layer, group):
        return mid_gain[layer, :, lanes(group * 1024 + core * 512, 512)]

    def add_vec(layer, row, value, span=slice(None)):
        vec[layer, row : row + 1, span] += value

    def weight_grad(left, left_spec, right, right_spec, target, target_spec):
        def body(left_ref, right_ref, out_ref):
            a = left_ref[...].reshape(left_ref.shape[-2:])
            b = right_ref[...].reshape(right_ref.shape[-2:])
            value = lax.dot_general(a, b, (((0,), (0,)), ((), ())), preferred_element_type=F32)
            out_ref[...] = value.astype(BF16).reshape(out_ref.shape)

        stage(body, [(left, left_spec), (right, right_spec)], [(target, target_spec)])

    def narrow_stage(layer, grad):
        own_half, make = saved[layer], made[layer]

        def body(c_ref, g_ref, own_ref, other_ref, w_ref, dm_ref):
            mean, scale = mid_stats(own_ref[...], other_ref[...])
            grad_low = c_ref[...]
            first = jnp.zeros((TILE, 1), F32)
            second = jnp.zeros((TILE, 1), F32)
            for group in range(4):
                d_middle = dot_nt(grad_low, w_ref[group])
                dm_ref[group] = d_middle.astype(BF16)
                unit_m = (g_ref[group].astype(F32) - mean) * scale
                product = d_middle * unit_m
                add_vec(layer, 6 + group, jnp.sum(product, axis=0, keepdims=True), column)
                add_vec(layer, 10 + group, jnp.sum(d_middle, axis=0, keepdims=True), column)
                row_gain = mid_row(layer, group)
                first = first + jnp.sum(d_middle * row_gain, axis=-1, keepdims=True)
                second = second + jnp.sum(product * row_gain, axis=-1, keepdims=True)
            swap_tile(layer * 3, sums[layer], two_columns(first, second))

        stage(
            body,
            [(grad, rows_spec(1024)), (own_half.gelu, group_spec(512)), (stats[layer][0], rows_spec(128)),
             (stats[layer][1], rows_spec(128)), (weights[layer][3], whole_spec((4, 512, 1024)))],
            [(make.d_middle, group_spec(512))],
        )

    def widen_stage(layer):
        own_half, make = saved[layer], made[layer]

        def body(dm_ref, g_ref, s_ref, own_ref, other_ref, a_ref, b_ref, w_ref, dh_ref):
            mean, scale = mid_stats(own_ref[...], other_ref[...])
            both = (a_ref[...] + b_ref[...]) * (1.0 / 4096)
            first, second = both[:, 0:1], both[:, 64:65]
            total = jnp.zeros((TILE, 1024), F32)
            for group in range(4):
                unit_m = (g_ref[group].astype(F32) - mean) * scale
                inner = dm_ref[group].astype(F32) * mid_row(layer, group)
                d_gelu = scale * (inner - first - unit_m * second)
                d_hidden = (d_gelu * s_ref[group].astype(F32)).astype(BF16)
                dh_ref[group] = d_hidden
                total = total + dot_nt(d_hidden, w_ref[group].reshape(1024, 512))
            swap_tile(layer * 3 + 1, swaps[0], total.astype(BF16))

        stage(
            body,
            [(make.d_middle, group_spec(512)), (own_half.gelu, group_spec(512)), (own_half.slope, group_spec(512)),
             (stats[layer][0], rows_spec(128)), (stats[layer][1], rows_spec(128)), (sums[layer][0], rows_spec(128)),
             (sums[layer][1], rows_spec(128)), (weights[layer][2], whole_spec((4, 4, 256, 512)))],
            [(make.d_hidden, group_spec(512))],
        )

    def norms_stage(layer, grad):
        own_half, make = saved[layer], made[layer]
        scale_row = jnp.concatenate(
            [head_row[layer, :, lanes(group * 256 + core * 128, 128)] for group in range(4)], axis=1
        )

        def body(c_ref, res_ref, da_ref, db_ref, ba_ref, bb_ref, ho_ref, w_ref, dr_ref, dbr_ref, dh_ref):
            unit_r, scale_r = standard(res_ref[...])
            d_ffn = da_ref[...].astype(F32) + db_ref[...].astype(F32)
            back, gain_third, shift_third = standard_back(unit_r, scale_r, gains[layer, 2:3, :], d_ffn)
            d_residual = c_ref[...].astype(F32) + back
            dr_ref[...] = d_residual
            unit_b, scale_b = standard(ba_ref[...].astype(F32) + bb_ref[...].astype(F32))
            back, gain_second, shift_second = standard_back(unit_b, scale_b, gains[layer, 1:2, :], d_residual)
            d_branch = back.astype(BF16)
            dbr_ref[...] = d_branch
            d_scaled = dot_nt(d_branch, w_ref[...].reshape(512, 1024))
            dh_ref[...] = (d_scaled * scale_row).astype(BF16)
            add_vec(layer, 14, jnp.sum(d_scaled * ho_ref[...].astype(F32), axis=0, keepdims=True), column)
            for row, value in ((1, gain_second), (2, gain_third), (4, shift_second), (5, shift_third)):
                add_vec(layer, row, value)

        stage(
            body,
            [(grad, rows_spec(1024)), (own_half.residual, rows_spec(1024)), (swaps[0][0], rows_spec(1024)),
             (swaps[0][1], rows_spec(1024)), (own_half.branch, rows_spec(1024)),
             (own_half.branch_other, rows_spec(1024)), (own_half.head_out, rows_spec(512)),
             (weights[layer][1], whole_spec((4, 128, 1024)))],
            [(make.d_residual, rows_spec(1024)), (make.d_branch, rows_spec(1024)), (make.d_heads, rows_spec(512))],
        )

    def attention_stage(layer):
        own_half, make = saved[layer], made[layer]

        def body(q_ref, k_ref, v_ref, grad_ref, out_ref, log_ref, back_ref):
            attend_back(
                q_ref, k_ref, v_ref, grad_ref, out_ref, log_ref, back_ref, split_ref[0], triangle, turned, walled, dk_acc, dv_acc
            )

        stage(
            body,
            [(own_half.proj, third_spec(0)), (own_half.proj, third_spec(1)), (own_half.proj, third_spec(2)),
             (make.d_heads, column_spec(128)), (own_half.head_out, column_spec(128)),
             (own_half.logs, pl.BlockSpec((1, 2, 1024), lambda group: (group, 0, 0)))],
            [(make.d_proj, block_spec(1024, 384))],
        )

    def project_stage(layer):
        make = made[layer]

        def body(d_ref, w_ref):
            total = dot_nt(d_ref[0], w_ref[0].reshape(1024, 384))
            for group in range(1, 4):
                total = total + dot_nt(d_ref[group], w_ref[group].reshape(1024, 384))
            swap_tile(layer * 3 + 2, swaps[1], total.astype(BF16))

        stage(
            body, [(make.d_proj, group_spec(384)), (weights[layer][0], whole_spec((4, 4, 256, 384)))], []
        )

    def entry_stage(layer):
        own_half, make = saved[layer], made[layer]

        def body(dr_ref, a_ref, b_ref, x_ref, dx_ref):
            unit_x, scale_x = standard(x_ref[...].astype(F32))
            d_normed = a_ref[...].astype(F32) + b_ref[...].astype(F32)
            back, gain_first, shift_first = standard_back(unit_x, scale_x, gains[layer, 0:1, :], d_normed)
            dx_ref[...] = (dr_ref[...] + back).astype(BF16)
            add_vec(layer, 0, gain_first)
            add_vec(layer, 3, shift_first)

        stage(
            body,
            [(make.d_residual, rows_spec(1024)), (swaps[1][0], rows_spec(1024)),
             (swaps[1][1], rows_spec(1024)), (own_half.entry, rows_spec(1024))],
            [(make.d_entry, rows_spec(1024))],
        )

    def layer_back(layer, grad, events):
        own_half, make = saved[layer], made[layer]
        base = 0 if layer == 1 else 4
        weight_grad(own_half.middle, block_spec(1024, 512), grad, whole_spec((1024, 1024)),
                    grads[layer][3], block_spec(512, 1024))
        events[0]()
        begin(base)
        if layer == 1:
            last_ready()
        narrow_stage(layer, grad)
        events[1]()
        swapped(layer * 3, sums[layer])
        widen_stage(layer)
        events[2]()
        weight_grad(own_half.ffn_input, whole_spec((1024, 1024)), make.d_hidden, block_spec(1024, 512),
                    grads[layer][2], grad_spec(512))
        begin(base + 1)
        swapped(layer * 3 + 1, swaps[0])
        norms_stage(layer, grad)
        events[3]()
        weight_grad(own_half.scaled, column_spec(128), make.d_branch, whole_spec((1024, 1024)),
                    grads[layer][1], block_spec(128, 1024))
        begin(base + 2)
        attention_stage(layer)
        events[4]()
        project_stage(layer)
        events[5]()
        weight_grad(own_half.normed, whole_spec((1024, 1024)), make.d_proj, block_spec(1024, 384),
                    grads[layer][0], grad_spec(384))
        begin(base + 3)
        swapped(layer * 3 + 2, swaps[1])
        entry_stage(layer)
        events[6]()

    def last_stage():
        def body(mid_ref, w_ref):
            total = dot(mid_ref[0], w_ref[0])
            for group in range(1, 4):
                total = total + dot(mid_ref[group], w_ref[group])
            swap_tile(6, swaps[2], total.astype(BF16))

        stage(body, [(saved[1].middle, group_spec(512)), (weights[1][3], whole_spec((4, 512, 1024)))], [])

    def output_stage():
        swapped(6, swaps[2])

        def body(res_ref, a_ref, b_ref, out_ref):
            out_ref[...] = (res_ref[...] + (a_ref[...].astype(F32) + b_ref[...].astype(F32))).astype(BF16)

        stage(
            body,
            [(saved[1].residual, rows_spec(1024)), (swaps[2][0], rows_spec(1024)), (swaps[2][1], rows_spec(1024))],
            [(output, rows_spec(1024))],
        )
        send_ends(1, output)

    def prepare():
        vec[...] = jnp.zeros_like(vec)

    layer_back(1, cotangent, (
        after((prepare,)),
        after(),
        after((second_hop, 0), (last_stage,)),
        after((deep_hop, 0), (output_stage,)),
        after((second_hop, 1), (finish, 0), (second_hop, 2)),
        after((deep_hop, 1), (forward, 0)),
        after((deep_hop, 2), (finish, 1), (corner, 0), (second_hop, 3)),
    ))
    layer_back(0, made[1].d_entry, (
        after((forward, 1), (finish, 2), (deep_hop, 3), (free_hops, 0)),
        after((corner, 1), (forward, 2)),
        after((second_hop, 4), (finish, 3), (free_hops, 1), (corner, 2)),
        after((deep_hop, 4), (forward, 3), (free_hops, 2)),
        after((second_hop, 5), (finish, 4), (corner, 3), (second_hop, 6)),
        after((deep_hop, 5), (forward, 4), (free_hops, 3)),
        after((deep_hop, 6),),
    ))
    send_ends(0, made[0].d_entry)
    small_step(0)
    second_hop(7)
    finish(5)
    finish(6)
    corner(4)
    small_take(0)
    small_step(1)
    deep_hop(7)
    forward(5)
    forward(6)
    small_take(1)
    small_step(2)
    finish(7)
    corner(5)
    corner(6)
    small_take(2)
    small_step(3)
    forward(7)
    small_take(3)
    small_step(4)
    corner(7)
    small_take(4)
    small_out[...] = acc[4]
    clean_up()
    for unit in range(8):
        clean(unit)
    for index in range(5):
        await_bytes(inbox.at[index], small_send.at[index])
    for step in range(4):
        await_bytes(ends.at[0], ends_send.at[step])
    for step in (1, 2, 3):
        await_bytes(ends.at[0], ends_recv.at[step])


def both_layers(split_at, items, weights, smalls):
    anywhere = pl.BlockSpec(memory_space=pl.ANY)
    local_space = pl.BlockSpec(memory_space=pltpu.VMEM)
    dma = pltpu.SemaphoreType.DMA
    rows, rows_wide = array((1024, 1024), BF16), array((1024, 1024), F32)
    weight_shapes = [
        array((4, 4, 256, 384), BF16),
        array((4, 128, 1024), BF16),
        array((4, 4, 256, 512), BF16),
        array((4, 512, 1024), BF16),
    ]
    wide, heads, proj = array((4, 1024, 512), BF16), array((1024, 512), BF16), array((4, 1024, 384), BF16)
    saved = [rows, rows, proj, heads, heads, array((4, 2, 1024), F32), rows, rows, rows_wide, rows, wide, wide, wide]
    made = [wide, wide, rows_wide, rows, heads, proj, rows]
    small_shapes = [(2,) + operand.shape for operand in smalls]
    shapes = [
        array((256, 3072), BF16),
        array((256, 1024), BF16),
        array((256, 4096), BF16),
        array((1024, 1024), BF16),
        array((4, 256, 1024), BF16),
        array((16, 1024), F32),
        rows,
        rows,
        *weight_shapes * 2,
        *saved * 2,
        *weight_shapes * 2,
        *made * 2,
    ]
    return pl.pallas_call(
        whole_kernel,
        in_specs=[pl.BlockSpec(memory_space=pltpu.SMEM)] + [anywhere] * 10,
        out_specs=[anywhere] * 5 + [local_space] + [anywhere] * (len(shapes) - 6),
        out_shape=shapes,
        scratch_shapes=[pltpu.VMEM(shape, F32) for shape in small_shapes]
        + [pltpu.VMEM((256, 256), F32), pltpu.VMEM((128, 1024), BF16), pltpu.VMEM((2, 1024, 128), BF16)]
        + [pltpu.VMEM((1024, 1024), BF16)] * 6
        + [pltpu.VMEM((1024, 128), F32)] * 8
        + [pltpu.VMEM((4, 2) + size, BF16) for size in SIZES]
        + [pltpu.VMEM((4, 2) + size, BF16) for size in SIZES]
        + [pltpu.VMEM((4,) + size, BF16) for size in SIZES]
        + [pltpu.VMEM((2, 3) + size, BF16) for size in SIZES]
        + [pltpu.VMEM((2, 16, 1024), F32), pltpu.VMEM((5, 16, 1024), F32), pltpu.VMEM((5, 16, 1024), F32)]
        + [pltpu.VMEM((1024, 128), F32), pltpu.VMEM((1024, 128), F32)]
        + [
            dma((2, 4)), dma((2, 4)), dma((2, 4)), dma((8, 2)), dma((8,)),
            dma((8,)), dma((8, 4)), dma((8,)), dma((8, 3, 3)), dma((3, 5)),
            dma((5,)), dma((5,)), dma((4,)),
        ]
        + [dma((8,))] * 7
        + [dma((8, 3)), dma((8,)), dma((8, 2, 4)), dma((4,)), dma((4,)), dma((5,)), dma((5,)), dma((7,)), dma((7,))]
        + [pltpu.SemaphoreType.REGULAR((4,))],
        compiler_params=pltpu.CompilerParams(
            collective_id=0, has_side_effects=True, vmem_limit_bytes=62 * 2**20
        ),
    )(split_at, items, *weights, *smalls)[:6]


def local(
    boundary,
    first_len,
    qkv_weight,
    out_weight,
    up_weight,
    down_weight,
    norm_gain,
    norm_shift,
    mid_gain,
    mid_shift,
    head_scale,
):
    split_at = pick(first_len, lax.axis_index("dp"))
    *shares, ends, totals = both_layers(
        split_at,
        boundary[0, :, 0],
        (qkv_weight[0], out_weight[0], up_weight[0], down_weight[0]),
        (norm_gain[0], norm_shift[0], mid_gain, mid_shift, jnp.repeat(head_scale, 64, axis=1)),
    )
    head_sums = jnp.sum(totals[14].reshape(2, 4, 2, 64), axis=3).transpose(1, 0, 2).reshape(1, 16)
    return (
        ends[None, :, None],
        *[share.astype(F32)[None] for share in shares],
        totals[0:3][None],
        totals[3:6][None],
        totals[6:10].reshape(1, 4096),
        totals[10:14].reshape(1, 4096),
        head_sums,
    )


def fits(mesh, boundary, mid_gain, head_scale):
    sizes = (mesh.shape["section"], mesh.shape["dp"], mesh.shape["shard"])
    return (
        sizes == (2, 4, 4)
        and boundary == (2, 4, 4, 1024, 1024)
        and mid_gain == (2, 4096)
        and head_scale == (2, 16)
    )


def solution(mesh):
    placed = (
        P("section", None, "shard", "dp", None),
        P(None, "shard"),
        P("section", "shard", None),
        P("section", "shard", None),
        P("section", "shard", None),
        P("section", "shard", None),
        P("section", None, None),
        P("section", None, None),
        P("section", None),
        P("section", None),
        P("section", None),
    )
    results = (
        P("section", None, "shard", "dp", None),
        P("section", "shard", None),
        P("section", "shard", None),
        P("section", "shard", None),
        P("section", "shard", None),
        P("section", None, None),
        P("section", None, None),
        P("section", None),
        P("section", None),
        P("section", None),
    )

    def whole(*arrays):
        fast = fits(mesh, arrays[0].shape, arrays[8].shape, arrays[10].shape)
        body = local if fast else general
        return jax.shard_map(
            body, mesh=mesh, in_specs=placed, out_specs=results, check_vma=False
        )(*arrays)

    return whole
```

profile of v0, /device:TPU:8, one launch (start us, length us, event | category | flops | bytes accessed | tf_op | source)
XLA Modules:
  0.0 553.3 jit_solution(8255681106204994523)
XLA Ops:
  0.6 0.0 copy-start
  0.7 0.6 copy-done
  1.3 0.6 constant_dynamic-slice_fusion
  1.9 0.7 broadcast_in_dim.38
  2.6 0.7 broadcast_in_dim.39.refs_10_
  3.3 1.3 copy_bitcast_fusion
  4.6 530.4 %shard_map.189 = (bf16[256,3072]{1,0:T(8,128)(2,1)}, bf16[256,1024]{1,0:T(8,128)(2,1)}, bf16[256,4096]{1,0:T(8,128)(2,1)}, bf16[1024,1024]{1,0:T(8,128)(2,1)}, b...) custom-call(s32[1]{0:T(128)} %bitcast.refs_0_, ...), custom_call_target="tpu_custom_call" | custom-call | tf_op jit(solution)/shard_map/pallas_call | solution.py:1470
  535.1 0.8 slice_reduce_fusion
  535.8 0.1 reshape_squeeze.3
  535.9 0.1 reduce_sum.9
  536.0 0.6 reshape.36
  536.6 0.8 slice_bitcast_fusion.2
  537.5 0.9 slice_bitcast_fusion
  538.4 0.6 copy.34
  539.0 0.6 copy.30
  539.6 0.6 copy.29
  540.2 0.6 copy.33
  540.9 0.0 copy-start.3
  540.9 2.3 bitcast_convert_fusion.3
  543.1 3.4 bitcast_convert_fusion.2
  546.6 0.0 copy-done.3
  546.6 0.0 copy-start.2
  546.6 2.5 bitcast_convert_fusion.1
  549.1 0.0 copy-done.2
  549.1 0.0 copy-start.4
  549.1 0.0 copy-start.1
  549.1 2.5 bitcast_convert_fusion
  551.6 0.0 copy-done.4
  551.6 1.3 copy.38
  552.9 0.0 copy-done.1
  (1 shorter events, 0.0 us)
Async XLA Ops:
  0.6 0.7 copy-start
  540.9 5.7 %copy-start.3 = (bf16[256,4096]{1,0:T(8,128)(2,1)S(1)}, bf16[256,4096]{1,0:T(8,128)(2,1)}, u32[]{:S(2)}) copy-start(bf16[256,4096]{1,0:T(8,128)(2,1)} %get-tuple-element.19) | copy-start | bytes 6291460
  546.6 2.5 copy-start.2
  549.1 2.5 copy-start.4
  549.1 3.8 copy-start.1
where the time goes:
time: 564 us; the launch traced here: 553 us
  Pallas kernels  530 us (94%)
  local copies, waits for them, and re-layouts  11 us (2%)
  other arithmetic  10.8 us (2%)
    pallas_call x1, Pallas kernels, both_layers(): pl.pallas_call(whole_kernel, in_specs=[pl.BlockSpec(memory_space=pltpu.SM...  530 us

commit v1 on v0

--- a/solution.py
+++ b/solution.py
@@ -276,10 +276,6 @@
     )
 
 
-def pick(value, index):
-    return lax.dynamic_index_in_dim(value, index, 0, keepdims=False)
-
-
 BF16 = jnp.bfloat16
 F32 = jnp.float32
 TILE = 256
@@ -763,7 +759,7 @@
         def body(q_ref, k_ref, v_ref, out_ref, scaled_ref, log_ref):
             scale_row = head_row[layer, :, lanes(pl.program_id(0) * 256 + core * 128, 128)]
             attend(
-                q_ref, k_ref, v_ref, scale_row, out_ref, scaled_ref, log_ref, split_ref[0], triangle, turned, walled
+                q_ref, k_ref, v_ref, scale_row, out_ref, scaled_ref, log_ref, split_ref[place], triangle, turned, walled
             )
 
         stage(
@@ -982,7 +978,8 @@
     items, *raw = take(5)
     small_in = take(5)
     shares = take(4)
-    (ends, small_out) = take(2)
+    (ends,) = take(1)
+    small_outs = take(5)
     cotangent, output = take(2)
     weights = (take(4), take(4))
     saved = [Saved(*take(13)) for unused in (0, 1)]
@@ -1284,7 +1281,7 @@
 
         def body(q_ref, k_ref, v_ref, grad_ref, out_ref, log_ref, back_ref):
             attend_back(
-                q_ref, k_ref, v_ref, grad_ref, out_ref, log_ref, back_ref, split_ref[0], triangle, turned, walled, dk_acc, dv_acc
+                q_ref, k_ref, v_ref, grad_ref, out_ref, log_ref, back_ref, split_ref[place], triangle, turned, walled, dk_acc, dv_acc
             )
 
         stage(
@@ -1386,47 +1383,55 @@
         vec[...] = jnp.zeros_like(vec)
 
     layer_back(1, cotangent, (
-        after((prepare,)),
+        after((prepare,),),
         after(),
-        after((second_hop, 0), (last_stage,)),
-        after((deep_hop, 0), (output_stage,)),
+        after((second_hop, 0),),
+        after((deep_hop, 0),),
         after((second_hop, 1), (finish, 0), (second_hop, 2)),
         after((deep_hop, 1), (forward, 0)),
-        after((deep_hop, 2), (finish, 1), (corner, 0), (second_hop, 3)),
+        after((deep_hop, 2), (corner, 0)),
     ))
     layer_back(0, made[1].d_entry, (
-        after((forward, 1), (finish, 2), (deep_hop, 3), (free_hops, 0)),
-        after((corner, 1), (forward, 2)),
-        after((second_hop, 4), (finish, 3), (free_hops, 1), (corner, 2)),
-        after((deep_hop, 4), (forward, 3), (free_hops, 2)),
-        after((second_hop, 5), (finish, 4), (corner, 3), (second_hop, 6)),
-        after((deep_hop, 5), (forward, 4), (free_hops, 3)),
-        after((deep_hop, 6),),
+        after((free_hops, 0),),
+        after((second_hop, 3), (finish, 1), (finish, 2)),
+        after((forward, 1), (forward, 2), (free_hops, 1)),
+        after((deep_hop, 3), (second_hop, 4), (corner, 1), (corner, 2), (free_hops, 2)),
+        after((deep_hop, 4), (finish, 3), (second_hop, 5), (second_hop, 6)),
+        after((forward, 3), (free_hops, 3)),
+        after((deep_hop, 5), (finish, 4), (corner, 3), (deep_hop, 6)),
     ))
-    send_ends(0, made[0].d_entry)
     small_step(0)
+    last_stage()
     second_hop(7)
+    output_stage()
+    forward(4)
     finish(5)
     finish(6)
-    corner(4)
     small_take(0)
     small_step(1)
     deep_hop(7)
+    send_ends(0, made[0].d_entry)
+    corner(4)
     forward(5)
     forward(6)
     small_take(1)
     small_step(2)
-    finish(7)
     corner(5)
     corner(6)
     small_take(2)
     small_step(3)
-    forward(7)
+    finish(7)
     small_take(3)
     small_step(4)
+    forward(7)
     corner(7)
     small_take(4)
-    small_out[...] = acc[4]
+    small_outs[0][0] = acc[4, 0:3, :]
+    small_outs[1][0] = acc[4, 3:6, :]
+    for group in range(4):
+        for row in (0, 1):
+            small_outs[2 + row][:, group * 1024 : group * 1024 + 1024] = acc[4, 6 + 4 * row + group : 7 + 4 * row + group, :]
+    small_outs[4][...] = acc[4, 14:15, :]
     clean_up()
     for unit in range(8):
         clean(unit)
@@ -1459,7 +1464,11 @@
         array((256, 4096), BF16),
         array((1024, 1024), BF16),
         array((4, 256, 1024), BF16),
-        array((16, 1024), F32),
+        array((1, 3, 1024), F32),
+        array((1, 3, 1024), F32),
+        array((1, 4096), F32),
+        array((1, 4096), F32),
+        array((1, 1024), F32),
         rows,
         rows,
         *weight_shapes * 2,
@@ -1470,7 +1479,7 @@
     return pl.pallas_call(
         whole_kernel,
         in_specs=[pl.BlockSpec(memory_space=pltpu.SMEM)] + [anywhere] * 10,
-        out_specs=[anywhere] * 5 + [local_space] + [anywhere] * (len(shapes) - 6),
+        out_specs=[anywhere] * 5 + [local_space] * 5 + [anywhere] * (len(shapes) - 10),
         out_shape=shapes,
         scratch_shapes=[pltpu.VMEM(shape, F32) for shape in small_shapes]
         + [pltpu.VMEM((256, 256), F32), pltpu.VMEM((128, 1024), BF16), pltpu.VMEM((2, 1024, 128), BF16)]
@@ -1493,7 +1502,7 @@
         compiler_params=pltpu.CompilerParams(
             collective_id=0, has_side_effects=True, vmem_limit_bytes=62 * 2**20
         ),
-    )(split_at, items, *weights, *smalls)[:6]
+    )(split_at, items, *weights, *smalls)[:10]
 
 
 def local(
@@ -1509,21 +1518,20 @@
     mid_shift,
     head_scale,
 ):
-    split_at = pick(first_len, lax.axis_index("dp"))
-    *shares, ends, totals = both_layers(
-        split_at,
-        boundary[0, :, 0],
+    *shares, ends, gain_sums, shift_sums, mid_gain_sums, mid_shift_sums, head_sums = both_layers(
+        first_len[:, 0],
+        boundary.reshape(4, 256, 1024),
         (qkv_weight[0], out_weight[0], up_weight[0], down_weight[0]),
         (norm_gain[0], norm_shift[0], mid_gain, mid_shift, jnp.repeat(head_scale, 64, axis=1)),
     )
-    head_sums = jnp.sum(totals[14].reshape(2, 4, 2, 64), axis=3).transpose(1, 0, 2).reshape(1, 16)
+    head_sums = jnp.sum(head_sums.reshape(2, 4, 2, 64), axis=3).transpose(1, 0, 2).reshape(1, 16)
     return (
         ends[None, :, None],
         *[share.astype(F32)[None] for share in shares],
-        totals[0:3][None],
-        totals[3:6][None],
-        totals[6:10].reshape(1, 4096),
-        totals[10:14].reshape(1, 4096),
+        gain_sums,
+        shift_sums,
+        mid_gain_sums,
+        mid_shift_sums,
         head_sums,
     )
 

time: 564 us -> 553 us (0.980)
  the two profiles are of different devices: /device:TPU:8 before, /device:TPU:16 now
where the time goes in v1:
time: 553 us; the launch traced here: 543 us
  Pallas kernels  524 us (95%)
  other arithmetic  10.6 us (2%)
  local copies, waits for them, and re-layouts  7.73 us (1%)
    pallas_call x1, Pallas kernels, both_layers(): pl.pallas_call(whole_kernel, in_specs=[pl.BlockSpec(memory_space=pltpu.SM...  524 us

profile of v1, /device:TPU:16, one launch (start us, length us, event | category | flops | bytes accessed | tf_op | source)
XLA Modules:
  0.0 543.1 jit_solution(14378309340219157438)
XLA Ops:
  0.6 1.3 copy_bitcast_fusion
  2.0 0.7 broadcast_in_dim.32
  2.7 0.7 broadcast_in_dim.33.refs_10_
  3.4 523.7 %shard_map.189 = (bf16[256,3072]{1,0:T(8,128)(2,1)}, bf16[256,1024]{1,0:T(8,128)(2,1)}, bf16[256,4096]{1,0:T(8,128)(2,1)}, bf16[1024,1024]{1,0:T(8,128)(2,1)}, b...) custom-call(s32[4]{0:T(128)} %bitcast.34, ...), custom_call_target="tpu_custom_call" | custom-call | tf_op jit(solution)/shard_map/pallas_call | solution.py:1479
  527.1 0.0 copy-start
  527.1 4.2 bitcast_convert_fusion
  531.3 0.0 copy-done
  531.3 0.0 copy-start.2
  531.3 2.5 bitcast_convert_fusion.1
  533.8 0.0 copy-start.3
  533.8 0.0 copy-done.2
  533.8 0.0 copy-start.8
  533.8 0.0 copy-start.5
  533.8 0.0 copy-start.4
  533.9 0.0 copy-start.1
  533.9 2.0 bitcast_convert_fusion.2
  535.9 0.0 copy-start.7
  535.9 0.0 copy-start.6
  535.9 0.0 copy-done.3
  535.9 1.1 bitcast_convert_fusion.3
  537.0 0.5 broadcast.6
  537.5 0.0 copy-done.8
  537.5 0.7 reduce.3
  538.2 0.1 reshape.35
  538.2 0.1 reduce_sum.9
  538.3 0.6 reshape.36
  538.9 0.0 copy-done.5
  538.9 0.6 copy.29
  539.6 0.0 copy-done.4
  539.6 0.6 copy.30
  540.2 0.0 copy-done.1
  540.2 1.3 copy.38
  541.5 0.0 copy-done.7
  541.5 0.6 copy.39
  542.1 0.0 copy-done.6
  542.1 0.6 copy.40
  (1 shorter events, 0.0 us)
Async XLA Ops:
  527.1 4.2 copy-start
  531.3 2.5 copy-start.2
  533.8 2.1 copy-start.3
  533.8 3.7 copy-start.8
  533.8 5.1 copy-start.5
  533.8 5.7 %copy-start.4 = (f32[1,3,1024]{2,1,0:T(4,128)S(1)}, f32[1,3,1024]{2,1,0:T(4,128)}, u32[]{:S(2)}) copy-start(f32[1,3,1024]{2,1,0:T(4,128)} %get-tuple-element.56) | copy-start | bytes 36868
  533.9 6.3 %copy-start.1 = (bf16[4,256,1024]{2,1,0:T(8,128)(2,1)S(1)}, bf16[4,256,1024]{2,1,0:T(8,128)(2,1)}, u32[]{:S(2)}) copy-start(bf16[4,256,1024]{2,1,0:T(8,128)(2,1)} %get-tuple-element.20) | copy-start | bytes 6291460
  535.9 5.6 %copy-start.7 = (f32[1,4096]{1,0:T(1,128)S(1)}, f32[1,4096]{1,0:T(1,128)}, u32[]{:S(2)}) copy-start(f32[1,4096]{1,0:T(1,128)} %get-tuple-element.79) | copy-start | bytes 49156
  535.9 6.2 %copy-start.6 = (f32[1,4096]{1,0:T(1,128)S(1)}, f32[1,4096]{1,0:T(1,128)}, u32[]{:S(2)}) copy-start(f32[1,4096]{1,0:T(1,128)} %get-tuple-element.80) | copy-start | bytes 49156

commit v2 on v1

--- a/solution.py
+++ b/solution.py
@@ -1348,11 +1348,16 @@
         begin(base + 2)
         attention_stage(layer)
         events[4]()
-        project_stage(layer)
-        events[5]()
+        if layer == 1:
+            project_stage(layer)
+            events[5]()
         weight_grad(own_half.normed, whole_spec((1024, 1024)), make.d_proj, block_spec(1024, 384),
                     grads[layer][0], grad_spec(384))
+        if layer == 0:
+            events[5]()
         begin(base + 3)
+        if layer == 0:
+            project_stage(layer)
         swapped(layer * 3 + 2, swaps[1])
         entry_stage(layer)
         events[6]()

time: 553 us -> 565 us (1.022)
  the two profiles are of different devices: /device:TPU:16 before, /device:TPU:8 now
where the time goes in v2:
time: 565 us; the launch traced here: 555 us
  Pallas kernels  535 us (95%)
  other arithmetic  10.6 us (2%)
  local copies, waits for them, and re-layouts  7.73 us (1%)
    pallas_call x1, Pallas kernels, both_layers(): pl.pallas_call(whole_kernel, in_specs=[pl.BlockSpec(memory_space=pltpu.SM...  535 us

profile of v2, /device:TPU:8, one launch (start us, length us, event | category | flops | bytes accessed | tf_op | source)
XLA Modules:
  0.0 554.6 jit_solution(18018953235672083286)
XLA Ops:
  0.6 1.3 copy_bitcast_fusion
  2.0 0.7 broadcast_in_dim.32
  2.7 0.7 broadcast_in_dim.33.refs_10_
  3.4 535.2 %shard_map.189 = (bf16[256,3072]{1,0:T(8,128)(2,1)}, bf16[256,1024]{1,0:T(8,128)(2,1)}, bf16[256,4096]{1,0:T(8,128)(2,1)}, bf16[1024,1024]{1,0:T(8,128)(2,1)}, b...) custom-call(s32[4]{0:T(128)} %bitcast.34, ...), custom_call_target="tpu_custom_call" | custom-call | tf_op jit(solution)/shard_map/pallas_call | solution.py:1484
  538.6 0.0 copy-start
  538.6 4.2 bitcast_convert_fusion
  542.8 0.0 copy-done
  542.8 0.0 copy-start.2
  542.8 2.5 bitcast_convert_fusion.1
  545.3 0.0 copy-start.3
  545.3 0.0 copy-done.2
  545.3 0.0 copy-start.8
  545.3 0.0 copy-start.5
  545.3 0.0 copy-start.4
  545.3 0.0 copy-start.1
  545.3 2.0 bitcast_convert_fusion.2
  547.4 0.0 copy-start.7
  547.4 0.0 copy-start.6
  547.4 0.0 copy-done.3
  547.4 1.1 bitcast_convert_fusion.3
  548.4 0.5 broadcast.6
  549.0 0.0 copy-done.8
  549.0 0.7 reduce.3
  549.6 0.1 reshape.35
  549.7 0.1 reduce_sum.9
  549.8 0.6 reshape.36
  550.4 0.0 copy-done.5
  550.4 0.6 copy.29
  551.0 0.0 copy-done.4
  551.0 0.6 copy.30
  551.6 0.0 copy-done.1
  551.6 1.3 copy.38
  553.0 0.0 copy-done.7
  553.0 0.6 copy.39
  553.6 0.0 copy-done.6
  553.6 0.6 copy.40
  (1 shorter events, 0.0 us)
Async XLA Ops:
  538.6 4.2 copy-start
  542.8 2.5 copy-start.2
  545.3 2.1 copy-start.3
  545.3 3.7 copy-start.8
  545.3 5.1 copy-start.5
  545.3 5.7 %copy-start.4 = (f32[1,3,1024]{2,1,0:T(4,128)S(1)}, f32[1,3,1024]{2,1,0:T(4,128)}, u32[]{:S(2)}) copy-start(f32[1,3,1024]{2,1,0:T(4,128)} %get-tuple-element.56) | copy-start | bytes 36868
  545.3 6.3 %copy-start.1 = (bf16[4,256,1024]{2,1,0:T(8,128)(2,1)S(1)}, bf16[4,256,1024]{2,1,0:T(8,128)(2,1)}, u32[]{:S(2)}) copy-start(bf16[4,256,1024]{2,1,0:T(8,128)(2,1)} %get-tuple-element.20) | copy-start | bytes 6291460
  547.4 5.6 %copy-start.7 = (f32[1,4096]{1,0:T(1,128)S(1)}, f32[1,4096]{1,0:T(1,128)}, u32[]{:S(2)}) copy-start(f32[1,4096]{1,0:T(1,128)} %get-tuple-element.79) | copy-start | bytes 49156
  547.4 6.2 %copy-start.6 = (f32[1,4096]{1,0:T(1,128)S(1)}, f32[1,4096]{1,0:T(1,128)}, u32[]{:S(2)}) copy-start(f32[1,4096]{1,0:T(1,128)} %get-tuple-element.80) | copy-start | bytes 49156
